TPU v7x, 32 devices: a whole 2x2x4 slice. The times are simulated.
32 devices in a mesh: groups: 2 (over y), seq: 4 (over z), head: 2 (over x), sub: 2 (over core).
Axes of the slice: x: 2, y: 2, z: 4, core: 2. Of those that a mesh axis runs over, the one named last changes fastest.
Arguments:
- hidden: bfloat16 [4096, 5376], P(('groups', 'seq'), 'sub'), parts along dimension 0, may hold values from -500 to 500
- norm_gain: float32 [5376], replicated, may hold values from 0.25 to 1.75
- w_query: bfloat16 [5376, 4096], P('seq', ('head', 'sub')), may hold values from -0.078125 to 0.078125
- w_key: bfloat16 [5376, 2048], P('seq', ('head', 'sub')), may hold values from -0.078125 to 0.078125
- w_value: bfloat16 [5376, 2048], P('seq', ('head', 'sub')), may hold values from -0.078125 to 0.078125
- query_gain: float32 [128], replicated, may hold values from 1 to 2.5
- key_gain: float32 [128], replicated, may hold values from 1 to 2.5
- block_source: int32 [32], P('groups'), parts along dimension 0, may hold values from 0 to 15, as said below
- block_doc: int32 [32], P('groups'), parts along dimension 0, may hold values from 0 to 3, never falling along the last dimension, each value on 1 to 8 neighbouring positions
Outputs:
- attention: bfloat16 [4096, 4096], P(('groups', 'seq'), ('head', 'sub')), parts along dimension 0
There are 2 independent parts, one for each index of `groups`. A program takes and returns all parts, laid end to end along the dimension named above; an argument that names none is the same for every part. Nothing has to cross between parts.
Inputs may be any that keep to these rules, and one draw needn't show every extreme that they name: block_source[b] is the arrival slot of block b, rows block_source[b] * 128 to block_source[b] * 128 + 127 of hidden, on shard block_source[b] // 4; each slot holds one block. Block b lies on its own shard b // 4 or on the shard just before or just after it. Of one shard's blocks at most 2 lie on each neighbouring shard, exactly as many as that neighbour's blocks lie on it, and in every draw some shard holds exactly 2 blocks of each of its two neighbours. `block_doc`: document ids never fall along the blocks; each document spans 1 to 8 blocks, one exactly 8.
All inputs are finite; a program needn't handle non-finite values.
Results may differ from a plain program's by a relative error of at most 0.012.
Values may be sent and summed in bfloat16 or wider, within the bound.
A program may use at most 128 MiB of HBM per device.

v0:
```python
import jax
import jax.numpy as jnp
from jax import lax
from jax.sharding import PartitionSpec as P

HEAD_DIM = 128
WINDOW = 1024
BLOCK = 128
CAP = 2


QUERY_SCALE = 168.0 ** (-0.5)
EPSILON = 1e-06
ROPE_BASE = 10000.0


def passed_along(x, axis, by):
    size = lax.axis_size(axis)
    pairs = [(i, i + by) for i in range(size) if 0 <= i + by < size]
    return lax.ppermute(x, axis, pairs)


def table_lookup(table, indices):
    hits = indices[:, None] == jnp.arange(table.shape[0], dtype=jnp.int32)[None, :]
    return jnp.sum(jnp.where(hits, table[None, :], 0), axis=1)


def token_positions(block_ids, block_doc):
    first_block = jnp.sum((block_doc[None, :] < block_doc[:, None]).astype(jnp.int32), axis=1)
    start_block = table_lookup(first_block, block_ids)
    within = jnp.arange(BLOCK, dtype=jnp.int32)
    return (
        ((block_ids - start_block)[:, None] * BLOCK + within[None, :])
        .reshape(-1)
        .astype(jnp.float32)
    )


def token_docs(token_ids, block_doc):
    return table_lookup(block_doc, jnp.floor_divide(token_ids, BLOCK))


def head_rotation(values, gain, positions, factor):
    token_count = values.shape[0]
    per_head = values.reshape(token_count, -1, HEAD_DIM)
    normed = (
        per_head * lax.rsqrt(jnp.mean(per_head * per_head, axis=2, keepdims=True) + EPSILON) * gain
    )
    half_dim = HEAD_DIM // 2
    frequency = ROPE_BASE ** (-(jnp.arange(half_dim, dtype=jnp.float32) * 2.0 / HEAD_DIM))
    angles = positions[:, None] * frequency[None, :]
    cosine = jnp.cos(angles)[:, None, :]
    sine_table = jnp.sin(angles)[:, None, :]
    first_half = normed[:, :, :half_dim]
    second_half = normed[:, :, half_dim:]
    turned = jnp.concatenate(
        [
            first_half * cosine - second_half * sine_table,
            second_half * cosine + first_half * sine_table,
        ],
        axis=2,
    )
    return (turned * factor).reshape(token_count, -1).astype(jnp.bfloat16)


def side_ranks(labels):
    length = labels.shape[0]
    earlier = jnp.arange(length)[None, :] < jnp.arange(length)[:, None]
    matching = labels[None, :] == labels[:, None]
    return jnp.sum((earlier & matching).astype(jnp.int32), axis=1)


def outgoing_slots(block_source, target, own_shard, block_count, shard_count):
    first_slot = jnp.clip(target, 0, shard_count - 1) * block_count
    slot_ids = lax.dynamic_slice_in_dim(block_source, first_slot, block_count)
    sending = (slot_ids // block_count == own_shard) & (target >= 0) & (target < shard_count)
    send_rank = side_ranks(sending.astype(jnp.int32))
    wanted = (jnp.arange(CAP)[:, None] == send_rank[None, :]) & sending[None, :]
    return jnp.sum(jnp.where(wanted, (slot_ids % block_count)[None, :], 0), axis=1)


def incoming_index(block_source, own_shard, block_count):
    slot_ids = lax.dynamic_slice_in_dim(block_source, own_shard * block_count, block_count)
    sides = slot_ids // block_count - own_shard
    side_rank = side_ranks(sides)
    from_prior = block_count + side_rank
    from_next = block_count + CAP + side_rank
    return jnp.where(
        sides == 0, slot_ids % block_count, jnp.where(sides < 0, from_prior, from_next)
    )


def migrate(values, block_source, own_shard, shard_count):
    row_count, col_count = values.shape
    block_count = row_count // BLOCK
    pieces = values.reshape(block_count, BLOCK, col_count)
    block_pool = [pieces]
    for offset in (1, -1):
        chosen = outgoing_slots(
            block_source, own_shard + offset, own_shard, block_count, shard_count
        )
        outgoing = jnp.take(pieces, chosen, axis=0)
        block_pool.append(passed_along(outgoing, "seq", offset))
    joined = jnp.concatenate(block_pool, axis=0)
    placed = jnp.take(joined, incoming_index(block_source, own_shard, block_count), axis=0)
    return placed.reshape(row_count, col_count)


def project_rows(halves, norm_gain, w_query, w_key, w_value, query_gain, key_gain, positions):
    full_rows = lax.all_gather(halves, "sub", axis=1, tiled=True)
    as_float = full_rows.astype(jnp.float32)
    normed = (
        as_float
        * lax.rsqrt(jnp.mean(as_float * as_float, axis=1, keepdims=True) + EPSILON)
        * norm_gain
    ).astype(jnp.bfloat16)
    segments = (
        lax.all_gather(w_query, "seq", axis=0, tiled=True),
        lax.all_gather(w_key, "seq", axis=0, tiled=True),
        lax.all_gather(w_value, "seq", axis=0, tiled=True),
    )
    query_raw, key_raw, value_raw = tuple(
        (jnp.dot(normed, segment, preferred_element_type=jnp.float32) for segment in segments)
    )
    query_rot = head_rotation(query_raw, query_gain, positions, QUERY_SCALE)
    key_rot = head_rotation(key_raw, key_gain, positions, 1.0)
    return jnp.concatenate([query_rot, key_rot, value_raw.astype(jnp.bfloat16)], axis=1)


def attend_block(query_rows, key_rows, value_rows, query_tokens, key_tokens, query_docs, key_docs):
    query_count = query_rows.shape[0]
    key_count = key_rows.shape[0]
    kv_count = key_rows.shape[1] // HEAD_DIM
    query_heads = query_rows.reshape(query_count, kv_count, 2, HEAD_DIM)
    key_heads = key_rows.reshape(key_count, kv_count, HEAD_DIM)
    value_heads = value_rows.reshape(key_count, kv_count, HEAD_DIM)
    scores = jnp.einsum(
        "qgjd,kgd->gjqk", query_heads, key_heads, preferred_element_type=jnp.float32
    )
    allowed = (key_tokens[None, :] >= 0) & (key_tokens[None, :] <= query_tokens[:, None])
    allowed = (
        allowed
        & (query_tokens[:, None] - key_tokens[None, :] < WINDOW)
        & (key_docs[None, :] == query_docs[:, None])
    )
    weight_exp = jnp.where(allowed, jnp.exp(scores), 0.0)
    totals = jnp.sum(weight_exp, axis=3)
    summed = jnp.einsum(
        "gjqk,kgd->qgjd",
        weight_exp.astype(jnp.bfloat16),
        value_heads,
        preferred_element_type=jnp.float32,
    )
    return (
        (summed / jnp.transpose(totals, (2, 0, 1))[:, :, :, None])
        .reshape(query_count, -1)
        .astype(jnp.bfloat16)
    )


def body(hidden, norm_gain, w_query, w_key, w_value, query_gain, key_gain, block_source, block_doc):
    row_count = hidden.shape[0]
    block_count = row_count // BLOCK
    own_shard = lax.axis_index("seq")
    shard_count = lax.axis_size("seq")
    own_blocks = own_shard * block_count + jnp.arange(block_count, dtype=jnp.int32)
    moved = migrate(hidden, block_source, own_shard, shard_count)
    packed = project_rows(
        moved,
        norm_gain,
        w_query,
        w_key,
        w_value,
        query_gain,
        key_gain,
        token_positions(own_blocks, block_doc),
    )
    query_width = w_query.shape[1]
    key_width = w_key.shape[1]
    query_rot = packed[:, :query_width]
    key_value = packed[:, query_width:]
    halo_count = max(1, WINDOW // row_count)
    received = []
    for distance in range(halo_count, 0, -1):
        received.append(passed_along(key_value, "seq", distance))
    extended = jnp.concatenate(received + [key_value], axis=0)
    key_all = extended[:, :key_width]
    value_all = extended[:, key_width:]
    query_tokens = own_shard * row_count + jnp.arange(row_count, dtype=jnp.int32)
    key_tokens = own_shard * row_count - WINDOW + jnp.arange(extended.shape[0], dtype=jnp.int32)
    query_docs = token_docs(query_tokens, block_doc)
    key_docs = token_docs(key_tokens, block_doc)
    block_rows = min(512, row_count)

    def one_block(block_index):
        return attend_block(
            query_rot, key_all, value_all, query_tokens, key_tokens, query_docs, key_docs
        )

    result = lax.map(one_block, jnp.arange(row_count // block_rows, dtype=jnp.int32))
    return result.reshape(row_count, -1)


def solution(mesh):
    placed = (
        P(("groups", "seq"), "sub"),
        P(),
        P("seq", ("head", "sub")),
        P("seq", ("head", "sub")),
        P("seq", ("head", "sub")),
        P(),
        P(),
        P("groups"),
        P("groups"),
    )
    return jax.shard_map(
        body,
        mesh=mesh,
        in_specs=placed,
        out_specs=P(("groups", "seq"), ("head", "sub")),
        check_vma=False,
    )
```

profile of v0, /device:TPU:8, one launch (start us, length us, event | category | flops | bytes accessed | tf_op | source)
XLA Modules:
  0.0 589.0 jit_solution(7441517687041226296)
XLA Ops:
  9.1 3.5 gather_fusion.2
  12.6 2.6 broadcast_select_fusion
  15.2 1.9 collective-permute-start.1
  20.6 3.9 collective-permute-start
  24.6 24.8 %collective-permute-done.1 = bf16[2,128,2688]{2,1,0:T(8,128)(2,1)} collective-permute-done((bf16[2,128,2688]{2,1,0:T(8,128)(2,1)}, bf16[2,128,2688]{2,1,0:T(8,128)(2,1)}, u32[]{:S(2)}, u32[]{:S(2)}) %collective-permute-start.1) | collective-permute-done | bytes 1376288 | tf_op jit(solution)/shard_map/ppermute | solution.py:20
  49.4 5.0 collective-permute-done
  54.4 4.2 pad_maximum_fusion
  58.5 3.5 gather_fusion
  62.1 2.2 bitcast_select_fusion.1
  68.1 14.6 %all-gather.5.cloned.1.call-done = bf16[512,5376]{1,0:T(8,128)(2,1)} async-done(((bf16[512,2688]{1,0:T(8,128)(2,1)}), bf16[512,5376]{1,0:T(8,128)(2,1)}) %all-gather.5.cloned.1.call-update) | async-done | bytes 5505040 | tf_op jit(solution)/shard_map/all_gather | solution.py:110
  82.7 3.7 fusion.6
  86.4 98.3 %all-gather.7.cloned.1.call-done = bf16[5376,512]{1,0:T(8,128)(2,1)} async-done(((bf16[1344,512]{1,0:T(8,128)(2,1)}), bf16[5376,512]{1,0:T(8,128)(2,1)}) %all-gather.7.cloned.1.call-update) | async-done | bytes 5505040 | tf_op jit(solution)/shard_map/all_gather | solution.py:119
  184.7 8.0 %multiply_reduce_fusion.1 = (f32[512,4]{0,1:T(4,128)S(1)}, f32[512,512]{0,1:T(8,128)S(1)}) fusion(bf16[5376,512]{1,0:T(8,128)(2,1)} %all-gather.7.cloned.1.call-done, bf16[512,5376]{1,0:T(8,128)(2,1)} %all-gather.5.cloned.1.call-done, f32[5376]{0:T(1024)S(1)} %copy-done.7, f32[512]{0:T(512)S(1)} %add_rsqrt_fusion.2), kind=kOutput, calls=%fused_computation.34 | convolution fusion | flops 2830104576 | bytes 12090368 | tf_op jit(solution)/shard_map/dot_general | solution.py:123
  193.2 93.9 %all-gather.9.cloned.1.call-done = bf16[5376,512]{1,0:T(8,128)(2,1)} async-done(((bf16[1344,512]{1,0:T(8,128)(2,1)}), bf16[5376,512]{1,0:T(8,128)(2,1)}) %all-gather.9.cloned.1.call-update) | async-done | bytes 5505040 | tf_op jit(solution)/shard_map/all_gather | solution.py:120
  287.1 7.3 %convolution_convert_fusion = bf16[512,512]{0,1:T(8,128)(2,1)S(1)} fusion(bf16[5376,512]{1,0:T(8,128)(2,1)} %all-gather.9.cloned.1.call-done, bf16[512,5376]{1,0:T(8,128)(2,1)} %all-gather.5.cloned.1.call-done, f32[5376]{0:T(1024)S(1)} %copy-done.7, f32[512]{0:T(512)S(1)} %add_rsqrt_fusion.2), kind=kOutput, calls=%fused_computation.31 | convolution fusion | flops 2829844480 | bytes 11557888 | tf_op jit(solution)/shard_map/dot_general | solution.py:123
  294.5 4.6 collective-permute-start.3
  300.9 2.6 fusion.10
  303.5 84.2 %collective-permute-done.3 = bf16[512,1024]{0,1:T(8,128)(2,1)S(1)} collective-permute-done((bf16[512,1024]{0,1:T(8,128)(2,1)S(1)}, bf16[512,1024]{0,1:T(8,128)(2,1)S(1)}, u32[]{:S(2)}, u32[]{:S(2)}) %collective-permute-start.3) | collective-permute-done | bytes 1048608 | tf_op jit(solution)/shard_map/ppermute | solution.py:20
  387.7 89.0 %collective-permute-done.2 = bf16[512,1024]{0,1:T(8,128)(2,1)S(1)} collective-permute-done((bf16[512,1024]{0,1:T(8,128)(2,1)S(1)}, bf16[512,1024]{0,1:T(8,128)(2,1)S(1)}, u32[]{:S(2)}, u32[]{:S(2)}) %collective-permute-start.2) | collective-permute-done | bytes 1048608 | tf_op jit(solution)/shard_map/ppermute | solution.py:20
  476.7 9.2 %maximum_maximum_fusion = bf16[1536,1024]{0,1:T(8,128)(2,1)S(1)} fusion(bf16[512,512]{0,1:T(8,128)(2,1)S(1)} %convolution_convert_fusion, bf16[512,512]{0,1:T(8,128)(2,1)S(1)} %bitcast.52, bf16[512,1024]{0,1:T(8,128)(2,1)S(1)} %collective-permute-done.3, bf16[512,1024]{0,1:T(8,128)(2,1)S(1)} %collective-permute-done.2), kind=kLoop, calls=%fused_computation.15 | loop fusion | flops 12582912 | bytes 6291456 | tf_op jit(solution)/shard_map/concatenate | solution.py:186
  487.8 55.9 %all-gather.11.cloned.1.call-done = bf16[5376,1024]{1,0:T(8,128)(2,1)} async-done(((bf16[1344,1024]{1,0:T(8,128)(2,1)}), bf16[5376,1024]{1,0:T(8,128)(2,1)}) %all-gather.11.cloned.1.call-update) | async-done | bytes 11010064 | tf_op jit(solution)/shard_map/all_gather | solution.py:118
  543.7 10.3 %convolution_bitcast_fusion = f32[64,8,8,128]{3,1,2,0:T(8,128)S(1)} fusion(bf16[5376,1024]{1,0:T(8,128)(2,1)} %all-gather.11.cloned.1.call-done, bf16[512,5376]{1,0:T(8,128)(2,1)} %all-gather.5.cloned.1.call-done, f32[5376]{0:T(1024)S(1)} %copy-done.7, f32[512]{0:T(512)S(1)} %add_rsqrt_fusion.2), kind=kOutput, calls=%fused_computation.28 | convolution fusion | flops 5648154624 | bytes 18635776 | tf_op jit(solution)/shard_map/dot_general | solution.py:123
  559.0 11.3 %fusion = (f32[4,2,512]{2,1,0:T(2,128)S(1)}, f32[4,1536,512,2]{2,1,3,0:T(8,128)}) fusion(pred[512,1536]{0,1:T(8,128)(4,1)S(1)} %copy-done.3, bf16[1536,4,128,1]{0,2,3,1:T(8,128)(2,1)S(1)} %bitcast.54, bf16[512,4,2,128]{3,0,2,1:T(8,128)(2,1)S(1)} %bitcast.55), kind=kOutput, calls=%fused_computation.4 | convolution fusion | flops 1623191552 | bytes 28590080 | tf_op jit(solution)/shard_map/while/body/eval_jaxpr/qgjd,kgd->gjqk/dot_general | solution.py:137
  570.4 10.7 %fusion.12 = bf16[512,4,2,128]{0,3,2,1:T(8,128)(2,1)S(1)} fusion(bf16[1536,4,128,1]{0,2,3,1:T(8,128)(2,1)S(1)} %bitcast.53, f32[4,1536,512,2]{2,1,3,0:T(8,128)} %get-tuple-element.57, pred[512,1536]{0,1:T(8,128)(4,1)S(1)} %copy-done.3, f32[512,4,2]{0,2,1:T(2,128)S(1)} %bitcast.57), kind=kOutput, calls=%fused_computation.23 | convolution fusion | flops 1624244224 | bytes 28590080 | tf_op jit(solution)/shard_map/while/body/eval_jaxpr/gjqk,kgd->qgjd/dot_general | solution.py:148
  (72 shorter events, 20.0 us)
Async XLA Ops:
  6.5 10.7 %copy-start = (bf16[512,2688]{1,0:T(8,128)(2,1)S(1)}, bf16[512,2688]{1,0:T(8,128)(2,1)}, u32[]{:S(2)}) copy-start(bf16[512,2688]{1,0:T(8,128)(2,1)} %param.11) | copy-start | bytes 8257540
  6.5 76.2 %all-gather.5.cloned.1.call-start = ((), (), s32[]{:S(2)}) async-start(), calls=%async_computation | async-start | bytes 8257536 | tf_op jit(solution)/shard_map/all_gather | solution.py:110
  15.2 34.1 %collective-permute-start.1 = (bf16[2,128,2688]{2,1,0:T(8,128)(2,1)}, bf16[2,128,2688]{2,1,0:T(8,128)(2,1)}, u32[]{:S(2)}, u32[]{:S(2)}) collective-permute-start(bf16[2,128,2688]{2,1,0:T(8,128)(2,1)} %broadcast_select_fusion), channel_id=1, source_target_pairs={{4,0},{8,4},{12,8},{5,1},{9,5},{13,9},{6,2},{10,6},{14,10},{7,3},{... | collective-permute-start | bytes 4128776 | tf_op jit(solution)/shard_map/ppermute | solution.py:20
  20.6 33.8 %collective-permute-start = (bf16[2,128,2688]{2,1,0:T(8,128)(2,1)S(1)}, bf16[2,128,2688]{2,1,0:T(8,128)(2,1)S(1)}, u32[]{:S(2)}, u32[]{:S(2)}) collective-permute-start(bf16[2,128,2688]{2,1,0:T(8,128)(2,1)S(1)} %broadcast_select_fusion.1), channel_id=1, source_target_pairs={{0,4},{4,8},{8,12},{1,5},{5,9},{9,13},{2,6},{6,10},{10,14},{3,7},{... | collective-permute-start | bytes 4128776 | tf_op jit(solution)/shard_map/ppermute | solution.py:20
  64.3 2.1 copy-start.4
  64.3 120.4 %all-gather.7.cloned.1.call-start = ((), (), s32[]{:S(2)}) async-start(), calls=%async_computation.1 | async-start | bytes 6881280 | tf_op jit(solution)/shard_map/all_gather | solution.py:119
  65.0 222.0 %all-gather.9.cloned.1.call-start = ((), (), s32[]{:S(2)}) async-start(), calls=%async_computation.2 | async-start | bytes 6881280 | tf_op jit(solution)/shard_map/all_gather | solution.py:120
  65.8 478.0 %all-gather.11.cloned.1.call-start = ((), (), s32[]{:S(2)}) async-start(), calls=%async_computation.3 | async-start | bytes 13762560 | tf_op jit(solution)/shard_map/all_gather | solution.py:118
  67.8 116.9 %copy-start.7 = (f32[5376]{0:T(1024)S(1)}, f32[5376]{0:T(1024)}, u32[]{:S(2)}) copy-start(f32[5376]{0:T(1024)} %param.12) | copy-start | bytes 64516
  86.4 106.3 %copy-start.5 = (f32[128]{0:T(128)S(1)}, f32[128]{0:T(128)}, u32[]{:S(2)}) copy-start(f32[128]{0:T(128)} %param.17) | copy-start | bytes 1540
  294.5 93.3 %collective-permute-start.3 = (bf16[512,1024]{0,1:T(8,128)(2,1)S(1)}, bf16[512,1024]{0,1:T(8,128)(2,1)S(1)}, u32[]{:S(2)}, u32[]{:S(2)}) collective-permute-start(bf16[512,1024]{0,1:T(8,128)(2,1)S(1)} %pad_maximum_fusion.1), channel_id=1, source_target_pairs={{0,4},{4,8},{8,12},{1,5},{5,9},{9,13},{2,6},{6,10},{10,14},{3,7},{... | collective-permute-start | bytes 3145736 | tf_op jit(solution)/shard_map/ppermute | solution.py:20
  299.1 177.6 %collective-permute-start.2 = (bf16[512,1024]{0,1:T(8,128)(2,1)S(1)}, bf16[512,1024]{0,1:T(8,128)(2,1)S(1)}, u32[]{:S(2)}, u32[]{:S(2)}) collective-permute-start(bf16[512,1024]{0,1:T(8,128)(2,1)S(1)} %pad_maximum_fusion.1), channel_id=1, source_target_pairs={{0,8},{4,12},{1,9},{5,13},{2,10},{6,14},{3,11},{7,15},{16,24},{20,... | collective-permute-start | bytes 3145736 | tf_op jit(solution)/shard_map/ppermute | solution.py:20
  554.1 1.4 copy-start.6
  557.4 1.4 copy-start.2
  557.4 1.6 copy-start.3
  559.0 11.3 %copy-start.1 = (bf16[1536,512]{0,1:T(8,128)(2,1)S(1)}, bf16[1536,512]{0,1:T(8,128)(2,1)}, u32[]{:S(2)}) copy-start(bf16[1536,512]{0,1:T(8,128)(2,1)} %get-tuple-element.40) | copy-start | bytes 4718596
Sparse Core Ops, SparseCore 0:
  64.4 18.2 all-gather.4
  84.3 100.4 all-gather.6
  186.3 100.7 all-gather.8
  288.5 255.2 all-gather.10
where the time goes:
time: 591 us; the launch traced here: 589 us
  waiting for transfers between devices  468 us (79%)
  matrix products  47.7 us (8%)
  other arithmetic  33.9 us (6%)
  local copies, waits for them, and re-layouts  14 us (2%)
  between operations  13.5 us (2%)
  starting transfers between devices  12.1 us (2%)
    ppermute x4, waiting for transfers between devices, passed_along(): return lax.ppermute(x, axis, pairs)  203 us
    all_gather x1, waiting for transfers between devices, project_rows(): lax.all_gather(w_key, 'seq', axis=0, tiled=True)  98.3 us
    all_gather x1, waiting for transfers between devices, project_rows(): lax.all_gather(w_value, 'seq', axis=0, tiled=True)  93.9 us
    all_gather x1, waiting for transfers between devices, project_rows(): lax.all_gather(w_query, 'seq', axis=0, tiled=True)  55.9 us
    dot_general x3, matrix products, project_rows(): jnp.dot(normed, segment, preferred_element_type=jnp.float32)  25.7 us
    all_gather x1, waiting for transfers between devices, project_rows(): full_rows = lax.all_gather(halves, 'sub', axis=1, tiled=True)  14.6 us
    ppermute x4, starting transfers between devices, passed_along(): return lax.ppermute(x, axis, pairs)  12 us
  transfers between devices with their start and end apart: 8, of which 8 were waited for; matrix products, arithmetic and copies ran while one was open for 7% of the time, Pallas kernels for 0%

commit v1 on v0

--- a/solution.py
+++ b/solution.py
@@ -1,6 +1,10 @@
+import functools
+
 import jax
 import jax.numpy as jnp
 from jax import lax
+from jax.experimental import pallas as pl
+from jax.experimental.pallas import tpu as pltpu
 from jax.sharding import PartitionSpec as P
 
 HEAD_DIM = 128
@@ -90,6 +94,13 @@
     )
 
 
+def blocks_at(pieces, chosen):
+    picked = [
+        lax.dynamic_slice_in_dim(pieces, chosen[i], 1, 0) for i in range(chosen.shape[0])
+    ]
+    return jnp.concatenate(picked, axis=0)
+
+
 def migrate(values, block_source, own_shard, shard_count):
     row_count, col_count = values.shape
     block_count = row_count // BLOCK
@@ -99,15 +110,31 @@
         chosen = outgoing_slots(
             block_source, own_shard + offset, own_shard, block_count, shard_count
         )
-        outgoing = jnp.take(pieces, chosen, axis=0)
+        outgoing = blocks_at(pieces, chosen)
         block_pool.append(passed_along(outgoing, "seq", offset))
     joined = jnp.concatenate(block_pool, axis=0)
-    placed = jnp.take(joined, incoming_index(block_source, own_shard, block_count), axis=0)
+    placed = blocks_at(joined, incoming_index(block_source, own_shard, block_count))
     return placed.reshape(row_count, col_count)
 
 
+def gathered(x, axis, dim):
+    size = lax.axis_size(axis)
+    index = lax.axis_index(axis)
+    extent = x.shape[dim]
+    shape = list(x.shape)
+    shape[dim] = extent * size
+    whole = jnp.zeros(shape, x.dtype)
+    pairs = [(i, (i + 1) % size) for i in range(size)]
+    for step in range(size):
+        owner = lax.rem(index + size - step, size)
+        whole = lax.dynamic_update_slice_in_dim(whole, x, owner * extent, dim)
+        if step < size - 1:
+            x = lax.ppermute(x, axis, pairs)
+    return whole
+
+
 def project_rows(halves, norm_gain, w_query, w_key, w_value, query_gain, key_gain, positions):
-    full_rows = lax.all_gather(halves, "sub", axis=1, tiled=True)
+    full_rows = gathered(halves, "sub", 1)
     as_float = full_rows.astype(jnp.float32)
     normed = (
         as_float
@@ -115,9 +142,9 @@
         * norm_gain
     ).astype(jnp.bfloat16)
     segments = (
-        lax.all_gather(w_query, "seq", axis=0, tiled=True),
-        lax.all_gather(w_key, "seq", axis=0, tiled=True),
-        lax.all_gather(w_value, "seq", axis=0, tiled=True),
+        gathered(w_query, "seq", 0),
+        gathered(w_key, "seq", 0),
+        gathered(w_value, "seq", 0),
     )
     query_raw, key_raw, value_raw = tuple(
         (jnp.dot(normed, segment, preferred_element_type=jnp.float32) for segment in segments)
@@ -201,6 +228,434 @@
     return result.reshape(row_count, -1)
 
 
+MESH = pl.DeviceIdType.MESH
+CHUNKS = 4
+VMEM_LIMIT = 48 * 1024 * 1024
+
+
+def remote(src, dst, send_sem, recv_sem, **target):
+    return pltpu.make_async_remote_copy(
+        src_ref=src,
+        dst_ref=dst,
+        send_sem=send_sem,
+        recv_sem=recv_sem,
+        device_id=target,
+        device_id_type=MESH,
+    )
+
+
+def gather_kernel(
+    shards, own_rows, wq, wk, wv, rows, weights,
+    zr_send, zr_recv, zl_send, zl_recv, x_send, x_recv, c_send, c_recv,
+    w_send, w_recv, y_send, y_recv, own_sem, ownw_sem,
+):
+    y, z = lax.axis_index("groups"), lax.axis_index("seq")
+    x, c = lax.axis_index("head"), lax.axis_index("sub")
+    chunks = own_rows.shape[1]
+    widths = (wq.shape[2] // shards, wk.shape[2] // shards, wv.shape[2] // shards)
+    starts = (0, widths[0], widths[0] + widths[1])
+
+    barrier = pltpu.get_barrier_semaphore()
+    for d in range(1, shards):
+        pl.semaphore_signal(
+            barrier, inc=1, device_id={"seq": lax.rem(z + d, shards)}, device_id_type=MESH
+        )
+    pl.semaphore_signal(barrier, inc=1, device_id={"groups": 1 - y}, device_id_type=MESH)
+    pl.semaphore_signal(barrier, inc=1, device_id={"head": 1 - x}, device_id_type=MESH)
+    pl.semaphore_signal(barrier, inc=1, device_id={"sub": 1 - c}, device_id_type=MESH)
+    pl.semaphore_wait(barrier, shards + 2)
+
+    def along(step, j, right):
+        s = z - step if right else z + step
+        src = own_rows.at[x, j] if step == 0 else rows.at[s, c, x, j]
+        send, recv = (zr_send, zr_recv) if right else (zl_send, zl_recv)
+        return remote(
+            src, rows.at[s, c, x, j], send.at[step, j], recv.at[step + 1, j],
+            seq=z + 1 if right else z - 1,
+        )
+
+    def along_recv(step, j, right):
+        s = z - step if right else z + step
+        send, recv = (zr_send, zr_recv) if right else (zl_send, zl_recv)
+        return remote(
+            rows.at[s, c, x, j], rows.at[s, c, x, j], send.at[0, j], recv.at[step, j],
+            seq=z - 1 if right else z + 1,
+        )
+
+    def across(s, j, half):
+        return remote(
+            rows.at[s, c, half, j], rows.at[s, c, half, j], x_send.at[s, j], x_recv.at[s, j],
+            head=1 - x,
+        )
+
+    def to_core(s, half, j, own=False):
+        src = own_rows.at[half, j] if own else rows.at[s, c, half, j]
+        return remote(
+            src, rows.at[s, c, half, j], c_send.at[s, half, j], c_recv.at[s, half, j], sub=1 - c
+        )
+
+    def from_core(s, half, j):
+        where = rows.at[s, 1 - c, half, j]
+        return remote(where, where, c_send.at[s, half, j], c_recv.at[s, half, j], sub=1 - c)
+
+    def weight_piece(d, n):
+        t = lax.rem(z + d, shards)
+        src = (wq, wk, wv)[n].at[y, :, pl.ds(pl.multiple_of(t * widths[n], widths[n]), widths[n])]
+        return remote(
+            src, weights.at[z, y, :, pl.ds(starts[n], widths[n])],
+            w_send.at[d, n], w_recv.at[d, n], seq=t,
+        )
+
+    def weight_arrival(d, n):
+        s = lax.rem(z + shards - d, shards)
+        where = weights.at[s, y, :, pl.ds(starts[n], widths[n])]
+        return remote(where, where, w_send.at[d, n], w_recv.at[d, n], seq=s)
+
+    def weight_across(d, half):
+        s = lax.rem(z + shards - d, shards)
+        where = weights.at[s, half]
+        return remote(where, where, y_send.at[d], y_recv.at[d], groups=1 - y)
+
+    def own_weight(n):
+        src = (wq, wk, wv)[n].at[:, :, pl.ds(pl.multiple_of(z * widths[n], widths[n]), widths[n])]
+        return pltpu.make_async_copy(
+            src, weights.at[z, :, :, pl.ds(starts[n], widths[n])], ownw_sem.at[n]
+        )
+
+    def own_copy():
+        return pltpu.make_async_copy(own_rows, rows.at[z, c], own_sem)
+
+    for j in range(chunks):
+        for right in (True, False):
+
+            @pl.when(z + 1 < shards if right else z > 0)
+            def _():
+                along(0, j, right).start()
+
+    for d in range(1, shards):
+        for n in range(3):
+            weight_piece(d, n).start()
+    for j in range(chunks):
+        to_core(z, 0, j, True).start()
+        to_core(z, 1, j, True).start()
+    own_copy().start()
+    for n in range(3):
+        own_weight(n).start()
+
+    def has(step, right):
+        return z - step >= 0 if right else z + step < shards
+
+    def second_hop(step, j):
+        for right in (True, False):
+
+            @pl.when(has(step, right))
+            def _():
+                s = z - step if right else z + step
+                across(s, j, 1 - x).wait_recv()
+                to_core(s, 1 - x, j).start()
+
+    order = [(step, j) for step in range(1, shards) for j in range(chunks)]
+    for i, (step, j) in enumerate(order):
+        for right in (True, False):
+
+            @pl.when(has(step, right))
+            def _():
+                s = z - step if right else z + step
+                along_recv(step, j, right).wait_recv()
+
+                @pl.when(z + 1 < shards if right else z > 0)
+                def _():
+                    along(step, j, right).start()
+
+                across(s, j, x).start()
+                to_core(s, x, j).start()
+
+        if j == chunks - 1:
+            for n in range(3):
+                weight_arrival(step, n).wait_recv()
+            weight_across(step, y).start()
+        if i > 0:
+            second_hop(*order[i - 1])
+    second_hop(*order[-1])
+
+    for d in range(1, shards):
+        weight_across(d, 1 - y).wait_recv()
+    for s in range(shards):
+        for half in range(2):
+            for j in range(chunks):
+                from_core(s, half, j).wait_recv()
+    own_copy().wait()
+    for n in range(3):
+        own_weight(n).wait()
+    for d in range(1, shards):
+        for n in range(3):
+            weight_piece(d, n).wait_send()
+        weight_across(d, y).wait_send()
+    for step in range(shards):
+        for right in (True, False):
+
+            @pl.when(has(step, right) & (z + 1 < shards if right else z > 0))
+            def _():
+                for j in range(chunks):
+                    along(step, j, right).wait_send()
+
+            if step > 0:
+
+                @pl.when(has(step, right))
+                def _():
+                    s = z - step if right else z + step
+                    for j in range(chunks):
+                        across(s, j, x).wait_send()
+    for s in range(shards):
+        for half in range(2):
+            for j in range(chunks):
+                to_core(s, half, j).wait_send()
+
+
+def gather_all(normed, w_query, w_key, w_value, shards):
+    row_count, width = normed.shape
+    depth = w_query.shape[0]
+    chunk = row_count // (2 * CHUNKS)
+    total = (w_query.shape[1] + w_key.shape[1] + w_value.shape[1]) // shards
+    halves = [w.reshape(2, depth // 2, w.shape[1]) for w in (w_query, w_key, w_value)]
+    dma = pltpu.SemaphoreType.DMA
+    line = dma((shards + 1, CHUNKS))
+    anywhere = pl.BlockSpec(memory_space=pl.ANY)
+    return pl.pallas_call(
+        functools.partial(gather_kernel, shards),
+        out_shape=(
+            jax.ShapeDtypeStruct((shards, 2, 2, CHUNKS, chunk, width), jnp.bfloat16),
+            jax.ShapeDtypeStruct((shards, 2, depth // 2, total), jnp.bfloat16),
+        ),
+        in_specs=[anywhere] * 4,
+        out_specs=(anywhere, anywhere),
+        scratch_shapes=[
+            line, line, line, line, line, line,
+            dma((shards, 2, CHUNKS)), dma((shards, 2, CHUNKS)),
+            dma((shards, 3)), dma((shards, 3)), dma((shards,)), dma((shards,)),
+            dma, dma((3,)),
+        ],
+        compiler_params=pltpu.CompilerParams(collective_id=0, has_side_effects=True),
+        name="gather_all",
+    )(normed.reshape(2, CHUNKS, chunk, width), *halves)
+
+
+def project_kernel(count, source, *refs):
+    xs = refs[:count]
+    weights, gains, cosine, sine, q_out, k_out, v_out = refs[count:]
+    width = xs[0].shape[-1]
+    low = jnp.concatenate([r[0, 0, 0] for r in xs], axis=0)
+    high = jnp.concatenate([r[0, 1, 0] for r in xs], axis=0)
+    acc = jnp.dot(low, weights[:width], preferred_element_type=jnp.float32)
+    acc = acc + jnp.dot(high, weights[width:], preferred_element_type=jnp.float32)
+
+    def turned(u, gain, factor):
+        n = u * lax.rsqrt(jnp.mean(u * u, axis=1, keepdims=True) + EPSILON) * gain
+        swapped = pltpu.roll(n, HEAD_DIM // 2, 1)
+        return ((n * cosine[...] + swapped * sine[...]) * factor).astype(jnp.bfloat16)
+
+    for h in range(2):
+        cols = slice(h * HEAD_DIM, (h + 1) * HEAD_DIM)
+        q_out[:, cols] = turned(acc[:, cols], gains[0:1, :], QUERY_SCALE)
+    k_out[...] = turned(acc[:, 2 * HEAD_DIM : 3 * HEAD_DIM], gains[1:2, :], 1.0)
+    v_out[...] = acc[:, 3 * HEAD_DIM :].astype(jnp.bfloat16)
+
+
+def project_all(rows, weights, gains, cosine, sine, block_source, per_shard):
+    count = 2
+    blocks = block_source.shape[0]
+    width = rows.shape[-1]
+    tokens = blocks * BLOCK
+    step = count * BLOCK
+
+    def picked(n):
+        def index(i, source):
+            slot = source[count * i + n]
+            return (slot // per_shard, 0, slot % per_shard, 0, 0)
+
+        return pl.BlockSpec((1, 2, 1, BLOCK, width), index)
+
+    return pl.pallas_call(
+        functools.partial(project_kernel, count),
+        grid_spec=pltpu.PrefetchScalarGridSpec(
+            num_scalar_prefetch=1,
+            grid=(blocks // count,),
+            in_specs=[picked(n) for n in range(count)]
+            + [
+                pl.BlockSpec(weights.shape, lambda i, source: (0, 0)),
+                pl.BlockSpec(gains.shape, lambda i, source: (0, 0)),
+                pl.BlockSpec((step, HEAD_DIM), lambda i, source: (i, 0)),
+                pl.BlockSpec((step, HEAD_DIM), lambda i, source: (i, 0)),
+            ],
+            out_specs=[
+                pl.BlockSpec((step, 2 * HEAD_DIM), lambda i, source: (i, 0)),
+                pl.BlockSpec((step, HEAD_DIM), lambda i, source: (i, 0)),
+                pl.BlockSpec((step, HEAD_DIM), lambda i, source: (i, 0)),
+            ],
+        ),
+        out_shape=(
+            jax.ShapeDtypeStruct((tokens, 2 * HEAD_DIM), jnp.bfloat16),
+            jax.ShapeDtypeStruct((tokens, HEAD_DIM), jnp.bfloat16),
+            jax.ShapeDtypeStruct((tokens, HEAD_DIM), jnp.bfloat16),
+        ),
+        compiler_params=pltpu.CompilerParams(vmem_limit_bytes=VMEM_LIMIT),
+        name="project_all",
+    )(block_source, *([rows] * count), weights, gains, cosine, sine)
+
+
+def attend_kernel(first, q_ref, k_ref, v_ref, out_ref):
+    b = pl.program_id(0)
+    span = 2 * BLOCK
+    query = jnp.concatenate([q_ref[:, :HEAD_DIM], q_ref[:, HEAD_DIM:]], axis=0)
+    start = first[b] * BLOCK
+    lowest = jnp.maximum(first[b], b - WINDOW // BLOCK)
+    token = b * BLOCK + lax.rem(lax.broadcasted_iota(jnp.int32, (span, span), 0), BLOCK)
+    lane = lax.broadcasted_iota(jnp.int32, (span, span), 1)
+    least = jnp.maximum(start, token - (WINDOW - 1))
+
+    def step(i, carry):
+        acc, total = carry
+        at = pl.multiple_of(i * span, span)
+        keys = k_ref[pl.ds(at, span), :]
+        scores = lax.dot_general(
+            query, keys, (((1,), (1,)), ((), ())), preferred_element_type=jnp.float32
+        )
+        other = lane + at
+        allowed = (other <= token) & (other >= least)
+        weight = jnp.where(allowed, jnp.exp(scores), 0.0)
+        total = total + weight[:, :HEAD_DIM] + weight[:, HEAD_DIM:]
+        acc = acc + jnp.dot(
+            weight.astype(jnp.bfloat16),
+            v_ref[pl.ds(at, span), :],
+            preferred_element_type=jnp.float32,
+        )
+        return acc, total
+
+    zero = jnp.zeros((span, HEAD_DIM), jnp.float32)
+    acc, total = lax.fori_loop(lowest // 2, b // 2 + 1, step, (zero, zero))
+    result = (acc / jnp.sum(total, axis=1, keepdims=True)).astype(jnp.bfloat16)
+    out_ref[:, :HEAD_DIM] = result[:BLOCK]
+    out_ref[:, HEAD_DIM:] = result[BLOCK:]
+
+
+def attend_all(query, key, value, first):
+    tokens = query.shape[0]
+    return pl.pallas_call(
+        attend_kernel,
+        grid_spec=pltpu.PrefetchScalarGridSpec(
+            num_scalar_prefetch=1,
+            grid=(tokens // BLOCK,),
+            in_specs=[
+                pl.BlockSpec((BLOCK, 2 * HEAD_DIM), lambda i, first: (i, 0)),
+                pl.BlockSpec(key.shape, lambda i, first: (0, 0)),
+                pl.BlockSpec(value.shape, lambda i, first: (0, 0)),
+            ],
+            out_specs=pl.BlockSpec((BLOCK, 2 * HEAD_DIM), lambda i, first: (i, 0)),
+        ),
+        out_shape=jax.ShapeDtypeStruct(query.shape, jnp.bfloat16),
+        compiler_params=pltpu.CompilerParams(vmem_limit_bytes=VMEM_LIMIT),
+        name="attend_all",
+    )(first, query, key, value)
+
+
+def scatter_kernel(shards, result, out, send, recv, own_sem):
+    z = lax.axis_index("seq")
+    rows, width = out.shape[0], result.shape[1]
+    barrier = pltpu.get_barrier_semaphore()
+    for d in range(1, shards):
+        pl.semaphore_signal(
+            barrier, inc=1, device_id={"seq": lax.rem(z + d, shards)}, device_id_type=MESH
+        )
+    pl.semaphore_wait(barrier, shards - 1)
+
+    def columns(s):
+        return out.at[:, pl.ds(pl.multiple_of(s * width, width), width)]
+
+    def part(t):
+        return result.at[pl.ds(pl.multiple_of(t * rows, rows), rows), :]
+
+    def outgoing(d):
+        t = lax.rem(z + d, shards)
+        return remote(part(t), columns(z), send.at[d], recv.at[d], seq=t)
+
+    def incoming(d):
+        s = lax.rem(z + shards - d, shards)
+        return remote(columns(s), columns(s), send.at[d], recv.at[d], seq=s)
+
+    own = pltpu.make_async_copy(part(z), columns(z), own_sem)
+    for d in range(1, shards):
+        outgoing(d).start()
+    own.start()
+    for d in range(1, shards):
+        incoming(d).wait_recv()
+    own.wait()
+    for d in range(1, shards):
+        outgoing(d).wait_send()
+
+
+def scatter_all(result, shards):
+    tokens, width = result.shape
+    dma = pltpu.SemaphoreType.DMA
+    anywhere = pl.BlockSpec(memory_space=pl.ANY)
+    return pl.pallas_call(
+        functools.partial(scatter_kernel, shards),
+        out_shape=jax.ShapeDtypeStruct((tokens // shards, width * shards), jnp.bfloat16),
+        in_specs=[anywhere],
+        out_specs=anywhere,
+        scratch_shapes=[dma((shards,)), dma((shards,)), dma],
+        compiler_params=pltpu.CompilerParams(collective_id=1, has_side_effects=True),
+        name="scatter_all",
+    )(result)
+
+
+def rotation_tables(positions):
+    half_dim = HEAD_DIM // 2
+    frequency = ROPE_BASE ** (-(jnp.arange(half_dim, dtype=jnp.float32) * 2.0 / HEAD_DIM))
+    angles = positions[:, None] * frequency[None, :]
+    cosine, sine = jnp.cos(angles), jnp.sin(angles)
+    return jnp.concatenate([cosine, cosine], axis=1), jnp.concatenate([-sine, sine], axis=1)
+
+
+def by_heads(
+    hidden, norm_gain, w_query, w_key, w_value, query_gain, key_gain, block_source, block_doc
+):
+    shards = lax.axis_size("seq")
+    width = hidden.shape[1]
+    blocks = block_source.shape[0]
+    as_float = hidden.astype(jnp.float32)
+    squares = jnp.sum(as_float * as_float, axis=1, keepdims=True)
+    others = lax.ppermute(squares, "sub", [(0, 1), (1, 0)])
+    gain = lax.dynamic_slice_in_dim(norm_gain, lax.axis_index("sub") * width, width)
+    normed = (
+        as_float * lax.rsqrt((squares + others) / (2 * width) + EPSILON) * gain[None, :]
+    ).astype(jnp.bfloat16)
+    first = jnp.sum((block_doc[None, :] < block_doc[:, None]).astype(jnp.int32), axis=1)
+    cosine, sine = rotation_tables(
+        token_positions(jnp.arange(blocks, dtype=jnp.int32), block_doc)
+    )
+    rows, weights = gather_all(normed, w_query, w_key, w_value, shards)
+    per_shard = blocks // shards
+    query, key, value = project_all(
+        rows.reshape(shards, 2, per_shard, BLOCK, width),
+        weights.reshape(2 * width, -1),
+        jnp.stack([query_gain, key_gain]),
+        cosine,
+        sine,
+        block_source,
+        per_shard,
+    )
+    return scatter_all(attend_all(query, key, value, first), shards)
+
+
+def fits(mesh):
+    return (
+        mesh.shape["groups"] == 2
+        and mesh.shape["head"] == 2
+        and mesh.shape["sub"] == 2
+        and mesh.shape["seq"] == 4
+    )
+
+
 def solution(mesh):
     placed = (
         P(("groups", "seq"), "sub"),
@@ -214,7 +669,7 @@
         P("groups"),
     )
     return jax.shard_map(
-        body,
+        by_heads if fits(mesh) else body,
         mesh=mesh,
         in_specs=placed,
         out_specs=P(("groups", "seq"), ("head", "sub")),

time: 591 us -> 234 us (0.40)
  waiting for transfers between devices: 468 us -> 0.01 us
  Pallas kernels: 0 us -> 219 us
  matrix products: 47.7 us -> 0 us
  other arithmetic: 33.9 us -> 12 us
  between operations: 13.5 us -> 0.12 us
  starting transfers between devices: 12.1 us -> 0.07 us
  local copies, waits for them, and re-layouts: 14 us -> 3.32 us
    all_gather x4 -> x0, waiting for transfers between devices: 263 us -> none  [the longest x1 98.3 us: project_rows(): lax.all_gather(w_key, 'seq', axis=0, tiled=True)]
    pallas_call x0 -> x4, Pallas kernels: none -> 219 us  [the longest x1 157 us: gather_all(): pl.pallas_call(functools.partial(gather_kernel, shards), out_shape=(jax.S...]
    ppermute x4 -> x1, waiting for transfers between devices: 203 us -> 0.01 us  [by_heads(): others = lax.ppermute(squares, 'sub', [(0, 1), (1, 0)])]
    dot_general x5 -> x0, matrix products: 47.7 us -> none  [the longest x3 25.7 us: project_rows(): jnp.dot(normed, segment, preferred_element_type=jnp.float32)]
    concatenate x4 -> x1, other arithmetic: 13.4 us -> 0.61 us  [rotation_tables(): jnp.concatenate([cosine, cosine], axis=1)]
    ppermute x4 -> x1, starting transfers between devices: 12 us -> 0.07 us  [by_heads(): others = lax.ppermute(squares, 'sub', [(0, 1), (1, 0)])]
    gather x3 -> x0, local copies, waits for them, and re-layouts: 8.84 us -> none  [the longest x2 5.34 us: migrate(): outgoing = jnp.take(pieces, chosen, axis=0)]
    select_n x7 -> x0, other arithmetic: 6.42 us -> none  [the longest x4 4.18 us: migrate(): outgoing = jnp.take(pieces, chosen, axis=0)]
  transfers between devices with their start and end apart: 8 -> 1, of which waited for: 8 -> 0; matrix products, arithmetic and copies ran while one was open for 7% -> 2% of each run, Pallas kernels for 0% -> 0%
where the time goes in v1:
time: 234 us
  Pallas kernels  219 us (94%)
  other arithmetic  12 us (5%)
  local copies, waits for them, and re-layouts  3.32 us (1%)
    pallas_call x1, Pallas kernels, gather_all(): pl.pallas_call(functools.partial(gather_kernel, shards), out_shape=(jax.S...  157 us
    pallas_call x1, Pallas kernels, scatter_all(): pl.pallas_call(functools.partial(scatter_kernel, shards), out_shape=jax.S...  25.4 us
    pallas_call x1, Pallas kernels, project_all(): pl.pallas_call(functools.partial(project_kernel, count), grid_spec=pltpu....  19.5 us
    pallas_call x1, Pallas kernels, attend_all(): pl.pallas_call(attend_kernel, grid_spec=pltpu.PrefetchScalarGridSpec(num_...  16.8 us
  transfers between devices with their start and end apart: 1, of which 0 were waited for; matrix products, arithmetic and copies ran while one was open for 2% of the time, Pallas kernels for 0%

profile of v1, /device:TPU:8, one launch (start us, length us, event | category | flops | bytes accessed | tf_op | source)
XLA Modules:
  0.0 234.0 jit_solution(13746386407538673670)
XLA Ops:
  0.0 0.0 copy-start.4
  0.0 0.0 copy-start.3
  0.0 0.0 copy-start.2
  0.0 2.4 %fusion = f32[512]{0:T(512)S(1)} fusion(bf16[512,2688]{1,0:T(8,128)(2,1)} %param.9), kind=kLoop, calls=%fused_computation.2 | loop fusion | flops 4128256 | bytes 2754560 | tf_op jit(solution)/shard_map/reduce_sum | solution.py:626
  2.4 0.1 collective-permute-start
  2.5 0.9 convert_reduce_fusion.first
  3.4 0.1 select_reduce_fusion
  3.6 0.1 convert_bitcast_fusion
  3.6 3.7 %fusion.3 = (f32[2048,64]{1,0:T(8,128)S(1)}, f32[2048,64]{1,0:T(8,128)S(1)}, f32[2048,64]{1,0:T(8,128)S(1)}) fusion(f32[64]{0:T(128)S(1)} %negate_power_fusion, f32[2048]{0:T(1024)S(1)} %convert_bitcast_fusion), kind=kLoop, calls=%fused_computation.9 | loop fusion | flops 262144 | bytes 1581312 | tf_op jit(solution)/shard_map/neg | solution.py:616
  7.4 0.6 pad_maximum_fusion
  8.0 0.0 copy-done.4
  8.0 0.0 copy-done.3
  8.0 0.0 copy-done.2
  8.0 0.1 dynamic_slice.3
  8.1 0.0 collective-permute-done
  8.1 4.1 %fusion.2 = bf16[512,2688]{1,0:T(8,128)(2,1)} fusion(bf16[512,2688]{1,0:T(8,128)(2,1)} %param.9, f32[2688]{0:T(1024)S(1)} %dynamic_slice.3, f32[512]{0:T(512)S(1)} %bitcast.21), kind=kLoop, calls=%fused_computation.4 | loop fusion | flops 5505024 | bytes 5517824 | tf_op jit(solution)/shard_map/convert_element_type | solution.py:631
  12.2 156.7 %gather_all.1 = (bf16[4,2,2,4,64,2688]{5,4,3,2,1,0:T(8,128)(2,1)}, bf16[4,2,672,512]{3,2,1,0:T(8,128)(2,1)}) custom-call(bf16[2,4,64,2688]{3,2,1,0:T(8,128)(2,1)} %bitcast.14, bf16[2,672,1024]{2,1,0:T(8,128)(2,1)} %bitcast.16, bf16[2,672,512]{2,1,0:T(8,128)(2,1)} %bitcast.17, bf16[2,672,512]{2,1,0:T(8,128)(2,1)} %bitcast.18), custom_call_target="tpu_custom_call" | custom-call | tf_op jit(solution)/shard_map/gather_all/pallas_call | solution.py:424
  168.9 0.0 copy-done.1
  168.9 19.5 %project_all.1 = (bf16[2048,256]{1,0:T(8,128)(2,1)S(1)}, bf16[2048,128]{1,0:T(8,128)(2,1)S(1)}, bf16[2048,128]{1,0:T(8,128)(2,1)S(1)}) custom-call(s32[16]{0:T(128)S(1)} %copy-done.1, bf16[4,2,4,128,2688]{4,3,2,1,0:T(8,128)(2,1)} %bitcast.12, bf16[4,2,4,128,2688]{4,3,2,1,0:T(8,128)(2,1)} %bitcast.13, bf16[5376,512]{1,0:T(8,128)(2,1)} %bitcast.15, ...), custom_call_target="tpu_custom_call" | custom-call | tf_op jit(solution)/shard_map/project_all/pallas_call | solution.py:478
  188.5 16.8 %attend_all.1.result = bf16[2048,256]{1,0:T(8,128)(2,1)S(1)} custom-call(s32[16]{0:T(128)S(1)} %convert_reduce_fusion.first, bf16[2048,256]{1,0:T(8,128)(2,1)S(1)} %get-tuple-element.12.q_ref, bf16[2048,128]{1,0:T(8,128)(2,1)S(1)} %get-tuple-element.13.k_ref, bf16[2048,128]{1,0:T(8,128)(2,1)S(1)} %get-tuple-element.14.v_ref), custom_call_target="tpu_custom_call" | custom-call | tf_op jit(solution)/shard_map/attend_all/pallas_call | solution.py:543
  205.3 0.0 copy-start
  205.3 1.0 copy-done
  206.3 25.4 %scatter_all.1 = bf16[512,1024]{1,0:T(8,128)(2,1)} custom-call(bf16[2048,256]{1,0:T(8,128)(2,1)} %copy-done), custom_call_target="tpu_custom_call" | custom-call | tf_op jit(solution)/shard_map/scatter_all/pallas_call | solution.py:600
  231.8 2.3 copy.11
  (5 shorter events, 0.0 us)
Async XLA Ops:
  0.0 8.0 %copy-start.4 = (f32[128]{0:T(128)S(1)}, f32[128]{0:T(128)}, u32[]{:S(2)}) copy-start(f32[128]{0:T(128)} %param.14) | copy-start | bytes 1540
  0.0 8.0 %copy-start.3 = (f32[128]{0:T(128)S(1)}, f32[128]{0:T(128)}, u32[]{:S(2)}) copy-start(f32[128]{0:T(128)} %param.15) | copy-start | bytes 1540
  0.0 8.0 %copy-start.2 = (f32[5376]{0:T(1024)S(1)}, f32[5376]{0:T(1024)}, u32[]{:S(2)}) copy-start(f32[5376]{0:T(1024)} %param.10) | copy-start | bytes 64516
  2.4 5.7 %collective-permute-start = (f32[512,1]{0,1:T(1,128)S(1)}, f32[512,1]{0,1:T(1,128)S(1)}, u32[]{:S(2)}, u32[]{:S(2)}) collective-permute-start(f32[512,1]{0,1:T(1,128)S(1)} %bitcast.19), channel_id=1, source_target_pairs={{0,1},{1,0},{2,3},{3,2},{4,5},{5,4},{6,7},{7,6},{8,9},{9,8},{10,11... | collective-permute-start | bytes 6152 | tf_op jit(solution)/shard_map/ppermute | solution.py:627
  12.2 156.7 %copy-start.1 = (s32[16]{0:T(128)S(1)}, s32[16]{0:T(128)}, u32[]{:S(2)}) copy-start(s32[16]{0:T(128)} %source.1) | copy-start | bytes 196
  205.3 1.0 copy-start

commit v2 on v1

--- a/solution.py
+++ b/solution.py
@@ -2,6 +2,7 @@
 
 import jax
 import jax.numpy as jnp
+import numpy as np
 from jax import lax
 from jax.experimental import pallas as pl
 from jax.experimental.pallas import tpu as pltpu
@@ -245,13 +246,14 @@
 
 
 def gather_kernel(
-    shards, own_rows, wq, wk, wv, rows, weights,
+    shards, hidden, norm_gain, gains, block_turn, within_turn, wq, wk, wv, out,
+    rows, weights, mine, theirs,
     zr_send, zr_recv, zl_send, zl_recv, x_send, x_recv, c_send, c_recv,
-    w_send, w_recv, y_send, y_recv, own_sem, ownw_sem,
+    w_send, w_recv, y_send, y_recv, ownw_sem, s_send, s_recv,
 ):
     y, z = lax.axis_index("groups"), lax.axis_index("seq")
     x, c = lax.axis_index("head"), lax.axis_index("sub")
-    chunks = own_rows.shape[1]
+    chunks, chunk, width = hidden.shape[1:]
     widths = (wq.shape[2] // shards, wk.shape[2] // shards, wv.shape[2] // shards)
     starts = (0, widths[0], widths[0] + widths[1])
 
@@ -267,10 +269,9 @@
 
     def along(step, j, right):
         s = z - step if right else z + step
-        src = own_rows.at[x, j] if step == 0 else rows.at[s, c, x, j]
         send, recv = (zr_send, zr_recv) if right else (zl_send, zl_recv)
         return remote(
-            src, rows.at[s, c, x, j], send.at[step, j], recv.at[step + 1, j],
+            rows.at[s, c, x, j], rows.at[s, c, x, j], send.at[step, j], recv.at[step + 1, j],
             seq=z + 1 if right else z - 1,
         )
 
@@ -288,11 +289,9 @@
             head=1 - x,
         )
 
-    def to_core(s, half, j, own=False):
-        src = own_rows.at[half, j] if own else rows.at[s, c, half, j]
-        return remote(
-            src, rows.at[s, c, half, j], c_send.at[s, half, j], c_recv.at[s, half, j], sub=1 - c
-        )
+    def to_core(s, half, j):
+        where = rows.at[s, c, half, j]
+        return remote(where, where, c_send.at[s, half, j], c_recv.at[s, half, j], sub=1 - c)
 
     def from_core(s, half, j):
         where = rows.at[s, 1 - c, half, j]
@@ -322,25 +321,41 @@
             src, weights.at[z, :, :, pl.ds(starts[n], widths[n])], ownw_sem.at[n]
         )
 
-    def own_copy():
-        return pltpu.make_async_copy(own_rows, rows.at[z, c], own_sem)
-
-    for j in range(chunks):
-        for right in (True, False):
-
-            @pl.when(z + 1 < shards if right else z > 0)
-            def _():
-                along(0, j, right).start()
+    def sums():
+        return remote(mine, theirs, s_send, s_recv, sub=1 - c)
 
     for d in range(1, shards):
         for n in range(3):
             weight_piece(d, n).start()
-    for j in range(chunks):
-        to_core(z, 0, j, True).start()
-        to_core(z, 1, j, True).start()
-    own_copy().start()
     for n in range(3):
         own_weight(n).start()
+
+    def add_up(i, _):
+        half, j = i // chunks, i % chunks
+        values = hidden[half, j].astype(jnp.float32)
+        total = jnp.sum(values * values, axis=1, keepdims=True)
+        mine[half, j] = jnp.broadcast_to(total, (chunk, HEAD_DIM))
+        return 0
+
+    lax.fori_loop(0, 2 * chunks, add_up, 0)
+    sums().start()
+    sums().wait_recv()
+
+    def normalise(i, _):
+        half, j = (x + i // chunks) % 2, i % chunks
+        mean = (mine[half, j][:, :1] + theirs[half, j][:, :1]) / (2 * width)
+        values = hidden[half, j].astype(jnp.float32) * lax.rsqrt(mean + EPSILON)
+        rows[z, c, half, j] = (values * norm_gain[pl.ds(c, 1), :]).astype(jnp.bfloat16)
+        for right in (True, False):
+
+            @pl.when((i < chunks) & (z + 1 < shards if right else z > 0))
+            def _():
+                along(0, j, right).start()
+
+        to_core(z, half, j).start()
+        return 0
+
+    lax.fori_loop(0, 2 * chunks, normalise, 0)
 
     def has(step, right):
         return z - step >= 0 if right else z + step < shards
@@ -354,8 +369,7 @@
                 across(s, j, 1 - x).wait_recv()
                 to_core(s, 1 - x, j).start()
 
-    order = [(step, j) for step in range(1, shards) for j in range(chunks)]
-    for i, (step, j) in enumerate(order):
+    def handle(step, j):
         for right in (True, False):
 
             @pl.when(has(step, right))
@@ -370,23 +384,67 @@
                 across(s, j, x).start()
                 to_core(s, x, j).start()
 
-        if j == chunks - 1:
-            for n in range(3):
-                weight_arrival(step, n).wait_recv()
-            weight_across(step, y).start()
-        if i > 0:
-            second_hop(*order[i - 1])
-    second_hop(*order[-1])
-
-    for d in range(1, shards):
-        weight_across(d, 1 - y).wait_recv()
-    for s in range(shards):
-        for half in range(2):
-            for j in range(chunks):
-                from_core(s, half, j).wait_recv()
-    own_copy().wait()
-    for n in range(3):
-        own_weight(n).wait()
+    def swap_weights(d):
+        for n in range(3):
+            weight_arrival(d, n).wait_recv()
+        weight_across(d, y).start()
+
+    def turned(u, gain, cosine, sine, factor):
+        n = u * lax.rsqrt(jnp.mean(u * u, axis=1, keepdims=True) + EPSILON) * gain
+        swapped = pltpu.roll(n, HEAD_DIM // 2, 1)
+        return ((n * cosine + swapped * sine) * factor).astype(jnp.bfloat16)
+
+    def project(i):
+        m, half = i // 2, i % 2
+        s = ((z // 2 + m // 2) % 2) * 2 + (z % 2 + m % 2) % 2
+        for j in range(chunks):
+            from_core(s, half, j).wait_recv()
+        acc = jnp.zeros((2 * BLOCK, 4 * HEAD_DIM), jnp.float32)
+        for part in range(2):
+            left = rows[s, part, half].reshape(2 * BLOCK, width)
+            right = weights[part * shards // 2 : (part + 1) * shards // 2]
+            acc = acc + jnp.dot(
+                left, right.reshape(width, 4 * HEAD_DIM), preferred_element_type=jnp.float32
+            )
+        for block in range(2):
+            slot = s * 4 + half * 2 + block
+            bc, bs = block_turn[0, pl.ds(slot, 1), :], block_turn[1, pl.ds(slot, 1), :]
+            wc, ws = within_turn[0], within_turn[1]
+            lane = lax.broadcasted_iota(jnp.int32, (BLOCK, HEAD_DIM), 1)
+            cosine = bc * wc - bs * ws
+            sine = jnp.where(lane < HEAD_DIM // 2, -1.0, 1.0) * (bs * wc + bc * ws)
+            at = pl.ds(pl.multiple_of(slot * BLOCK, BLOCK), BLOCK)
+            own = acc[block * BLOCK : (block + 1) * BLOCK]
+            for h in range(3):
+                cols = slice(h * HEAD_DIM, (h + 1) * HEAD_DIM)
+                gain, factor = (gains[0:1], QUERY_SCALE) if h < 2 else (gains[1:2], 1.0)
+                out[at, cols] = turned(own[:, cols], gain, cosine, sine, factor)
+            out[at, 3 * HEAD_DIM :] = own[:, 3 * HEAD_DIM :].astype(jnp.bfloat16)
+
+    for j in range(chunks):
+        handle(1, j)
+        if j > 0:
+            second_hop(1, j - 1)
+    swap_weights(1)
+
+    for n in range(2 * chunks + 2):
+        if n < 2 * chunks:
+            handle(2 + n // chunks, n % chunks)
+        if n < 2:
+            swap_weights(2 + n)
+        if n == 0:
+            second_hop(1, chunks - 1)
+        elif n <= 2 * chunks:
+            second_hop(2 + (n - 1) // chunks, (n - 1) % chunks)
+        if n == 2:
+            for d in range(1, shards):
+                weight_across(d, 1 - y).wait_recv()
+            for k in range(3):
+                own_weight(k).wait()
+        if n >= 2:
+            project(n - 2)
+
+    sums().wait_send()
     for d in range(1, shards):
         for n in range(3):
             weight_piece(d, n).wait_send()
@@ -412,8 +470,8 @@
                 to_core(s, half, j).wait_send()
 
 
-def gather_all(normed, w_query, w_key, w_value, shards):
-    row_count, width = normed.shape
+def gather_all(hidden, norm_gain, gains, block_turn, within_turn, w_query, w_key, w_value, shards):
+    row_count, width = hidden.shape
     depth = w_query.shape[0]
     chunk = row_count // (2 * CHUNKS)
     total = (w_query.shape[1] + w_key.shape[1] + w_value.shape[1]) // shards
@@ -421,90 +479,42 @@
     dma = pltpu.SemaphoreType.DMA
     line = dma((shards + 1, CHUNKS))
     anywhere = pl.BlockSpec(memory_space=pl.ANY)
+    inside = pl.BlockSpec(memory_space=pltpu.VMEM)
     return pl.pallas_call(
         functools.partial(gather_kernel, shards),
-        out_shape=(
-            jax.ShapeDtypeStruct((shards, 2, 2, CHUNKS, chunk, width), jnp.bfloat16),
-            jax.ShapeDtypeStruct((shards, 2, depth // 2, total), jnp.bfloat16),
-        ),
-        in_specs=[anywhere] * 4,
-        out_specs=(anywhere, anywhere),
+        out_shape=jax.ShapeDtypeStruct((row_count * shards, total), jnp.bfloat16),
+        in_specs=[inside] * 5 + [anywhere] * 3,
+        out_specs=inside,
         scratch_shapes=[
+            pltpu.VMEM((shards, 2, 2, CHUNKS, chunk, width), jnp.bfloat16),
+            pltpu.VMEM((shards, 2, depth // 2, total), jnp.bfloat16),
+            pltpu.VMEM((2, CHUNKS, chunk, HEAD_DIM), jnp.float32),
+            pltpu.VMEM((2, CHUNKS, chunk, HEAD_DIM), jnp.float32),
             line, line, line, line, line, line,
             dma((shards, 2, CHUNKS)), dma((shards, 2, CHUNKS)),
             dma((shards, 3)), dma((shards, 3)), dma((shards,)), dma((shards,)),
-            dma, dma((3,)),
+            dma((3,)), dma, dma,
         ],
-        compiler_params=pltpu.CompilerParams(collective_id=0, has_side_effects=True),
+        compiler_params=pltpu.CompilerParams(
+            collective_id=0, has_side_effects=True, vmem_limit_bytes=VMEM_LIMIT
+        ),
         name="gather_all",
-    )(normed.reshape(2, CHUNKS, chunk, width), *halves)
-
-
-def project_kernel(count, source, *refs):
-    xs = refs[:count]
-    weights, gains, cosine, sine, q_out, k_out, v_out = refs[count:]
-    width = xs[0].shape[-1]
-    low = jnp.concatenate([r[0, 0, 0] for r in xs], axis=0)
-    high = jnp.concatenate([r[0, 1, 0] for r in xs], axis=0)
-    acc = jnp.dot(low, weights[:width], preferred_element_type=jnp.float32)
-    acc = acc + jnp.dot(high, weights[width:], preferred_element_type=jnp.float32)
-
-    def turned(u, gain, factor):
-        n = u * lax.rsqrt(jnp.mean(u * u, axis=1, keepdims=True) + EPSILON) * gain
-        swapped = pltpu.roll(n, HEAD_DIM // 2, 1)
-        return ((n * cosine[...] + swapped * sine[...]) * factor).astype(jnp.bfloat16)
-
-    for h in range(2):
-        cols = slice(h * HEAD_DIM, (h + 1) * HEAD_DIM)
-        q_out[:, cols] = turned(acc[:, cols], gains[0:1, :], QUERY_SCALE)
-    k_out[...] = turned(acc[:, 2 * HEAD_DIM : 3 * HEAD_DIM], gains[1:2, :], 1.0)
-    v_out[...] = acc[:, 3 * HEAD_DIM :].astype(jnp.bfloat16)
-
-
-def project_all(rows, weights, gains, cosine, sine, block_source, per_shard):
-    count = 2
-    blocks = block_source.shape[0]
-    width = rows.shape[-1]
-    tokens = blocks * BLOCK
-    step = count * BLOCK
-
-    def picked(n):
-        def index(i, source):
-            slot = source[count * i + n]
-            return (slot // per_shard, 0, slot % per_shard, 0, 0)
-
-        return pl.BlockSpec((1, 2, 1, BLOCK, width), index)
-
-    return pl.pallas_call(
-        functools.partial(project_kernel, count),
-        grid_spec=pltpu.PrefetchScalarGridSpec(
-            num_scalar_prefetch=1,
-            grid=(blocks // count,),
-            in_specs=[picked(n) for n in range(count)]
-            + [
-                pl.BlockSpec(weights.shape, lambda i, source: (0, 0)),
-                pl.BlockSpec(gains.shape, lambda i, source: (0, 0)),
-                pl.BlockSpec((step, HEAD_DIM), lambda i, source: (i, 0)),
-                pl.BlockSpec((step, HEAD_DIM), lambda i, source: (i, 0)),
-            ],
-            out_specs=[
-                pl.BlockSpec((step, 2 * HEAD_DIM), lambda i, source: (i, 0)),
-                pl.BlockSpec((step, HEAD_DIM), lambda i, source: (i, 0)),
-                pl.BlockSpec((step, HEAD_DIM), lambda i, source: (i, 0)),
-            ],
-        ),
-        out_shape=(
-            jax.ShapeDtypeStruct((tokens, 2 * HEAD_DIM), jnp.bfloat16),
-            jax.ShapeDtypeStruct((tokens, HEAD_DIM), jnp.bfloat16),
-            jax.ShapeDtypeStruct((tokens, HEAD_DIM), jnp.bfloat16),
-        ),
-        compiler_params=pltpu.CompilerParams(vmem_limit_bytes=VMEM_LIMIT),
-        name="project_all",
-    )(block_source, *([rows] * count), weights, gains, cosine, sine)
-
-
-def attend_kernel(first, q_ref, k_ref, v_ref, out_ref):
+    )(
+        hidden.reshape(2, CHUNKS, chunk, width), norm_gain.reshape(2, width), gains,
+        block_turn, within_turn, *halves,
+    )
+
+
+def attend_kernel(first, source, q_ref, all_ref, out_ref, k_ref, v_ref):
     b = pl.program_id(0)
+
+    @pl.when(b == 0)
+    def _():
+        for i in range(k_ref.shape[0] // BLOCK):
+            at = pl.ds(pl.multiple_of(source[i] * BLOCK, BLOCK), BLOCK)
+            k_ref[i * BLOCK : (i + 1) * BLOCK, :] = all_ref[at, 2 * HEAD_DIM : 3 * HEAD_DIM]
+            v_ref[i * BLOCK : (i + 1) * BLOCK, :] = all_ref[at, 3 * HEAD_DIM :]
+
     span = 2 * BLOCK
     query = jnp.concatenate([q_ref[:, :HEAD_DIM], q_ref[:, HEAD_DIM:]], axis=0)
     start = first[b] * BLOCK
@@ -538,24 +548,27 @@
     out_ref[:, HEAD_DIM:] = result[BLOCK:]
 
 
-def attend_all(query, key, value, first):
-    tokens = query.shape[0]
+def attend_all(packed, first, source):
+    tokens = packed.shape[0]
     return pl.pallas_call(
         attend_kernel,
         grid_spec=pltpu.PrefetchScalarGridSpec(
-            num_scalar_prefetch=1,
+            num_scalar_prefetch=2,
             grid=(tokens // BLOCK,),
             in_specs=[
-                pl.BlockSpec((BLOCK, 2 * HEAD_DIM), lambda i, first: (i, 0)),
-                pl.BlockSpec(key.shape, lambda i, first: (0, 0)),
-                pl.BlockSpec(value.shape, lambda i, first: (0, 0)),
+                pl.BlockSpec((BLOCK, 2 * HEAD_DIM), lambda i, first, source: (source[i], 0)),
+                pl.BlockSpec(packed.shape, lambda i, first, source: (0, 0)),
             ],
-            out_specs=pl.BlockSpec((BLOCK, 2 * HEAD_DIM), lambda i, first: (i, 0)),
+            out_specs=pl.BlockSpec((BLOCK, 2 * HEAD_DIM), lambda i, first, source: (i, 0)),
+            scratch_shapes=[
+                pltpu.VMEM((tokens, HEAD_DIM), jnp.bfloat16),
+                pltpu.VMEM((tokens, HEAD_DIM), jnp.bfloat16),
+            ],
         ),
-        out_shape=jax.ShapeDtypeStruct(query.shape, jnp.bfloat16),
+        out_shape=jax.ShapeDtypeStruct((tokens, 2 * HEAD_DIM), jnp.bfloat16),
         compiler_params=pltpu.CompilerParams(vmem_limit_bytes=VMEM_LIMIT),
         name="attend_all",
-    )(first, query, key, value)
+    )(first, source, packed, packed)
 
 
 def scatter_kernel(shards, result, out, send, recv, own_sem):
@@ -608,43 +621,37 @@
     )(result)
 
 
-def rotation_tables(positions):
+def turn_table(positions):
     half_dim = HEAD_DIM // 2
-    frequency = ROPE_BASE ** (-(jnp.arange(half_dim, dtype=jnp.float32) * 2.0 / HEAD_DIM))
-    angles = positions[:, None] * frequency[None, :]
-    cosine, sine = jnp.cos(angles), jnp.sin(angles)
-    return jnp.concatenate([cosine, cosine], axis=1), jnp.concatenate([-sine, sine], axis=1)
+    frequency = ROPE_BASE ** (-(np.arange(half_dim, dtype=np.float64) * 2.0 / HEAD_DIM))
+    angles = np.asarray(positions, np.float64)[:, None] * np.tile(frequency, 2)[None, :]
+    return np.stack([np.cos(angles), np.sin(angles)]).astype(np.float32)
 
 
 def by_heads(
     hidden, norm_gain, w_query, w_key, w_value, query_gain, key_gain, block_source, block_doc
 ):
     shards = lax.axis_size("seq")
-    width = hidden.shape[1]
     blocks = block_source.shape[0]
-    as_float = hidden.astype(jnp.float32)
-    squares = jnp.sum(as_float * as_float, axis=1, keepdims=True)
-    others = lax.ppermute(squares, "sub", [(0, 1), (1, 0)])
-    gain = lax.dynamic_slice_in_dim(norm_gain, lax.axis_index("sub") * width, width)
-    normed = (
-        as_float * lax.rsqrt((squares + others) / (2 * width) + EPSILON) * gain[None, :]
-    ).astype(jnp.bfloat16)
+    ids = jnp.arange(blocks, dtype=jnp.int32)
     first = jnp.sum((block_doc[None, :] < block_doc[:, None]).astype(jnp.int32), axis=1)
-    cosine, sine = rotation_tables(
-        token_positions(jnp.arange(blocks, dtype=jnp.int32), block_doc)
-    )
-    rows, weights = gather_all(normed, w_query, w_key, w_value, shards)
-    per_shard = blocks // shards
-    query, key, value = project_all(
-        rows.reshape(shards, 2, per_shard, BLOCK, width),
-        weights.reshape(2 * width, -1),
+    arrived = block_source[None, :] == ids[:, None]
+    offset = jnp.sum(jnp.where(arrived, (ids - first)[None, :], 0), axis=1)
+    picked = (offset[:, None] == ids[None, :])[None, :, :, None]
+    table = jnp.asarray(turn_table(np.arange(blocks) * BLOCK))
+    block_turn = jnp.sum(jnp.where(picked, table[:, None, :, :], 0.0), axis=2)
+    packed = gather_all(
+        hidden,
+        norm_gain,
         jnp.stack([query_gain, key_gain]),
-        cosine,
-        sine,
-        block_source,
-        per_shard,
-    )
-    return scatter_all(attend_all(query, key, value, first), shards)
+        block_turn,
+        jnp.asarray(turn_table(np.arange(BLOCK))),
+        w_query,
+        w_key,
+        w_value,
+        shards,
+    )
+    return scatter_all(attend_all(packed, first, block_source), shards)
 
 
 def fits(mesh):

time: 234 us -> 236 us (level); the launches traced: 234 us -> 232 us
  other arithmetic: 12 us -> 3.29 us
  local copies, waits for them, and re-layouts: 3.32 us -> 7.56 us
    pallas_call x1, Pallas kernels: 25.4 us -> 30.9 us  [scatter_all(): pl.pallas_call(functools.partial(scatter_kernel, shards), out_shape=jax.S...]
    convert_element_type x2 -> x0, other arithmetic: 4.18 us -> none  [the longest x1 4.11 us: by_heads(): normed = (as_float * lax.rsqrt((squares + others) / (2 * width) + EPSILON...]
    neg x1 -> x0, other arithmetic: 3.73 us -> none  [rotation_tables(): -sine]
    unnamed x11, local copies, waits for them, and re-layouts: 3.24 us -> 6.81 us
    pallas_call x2 -> x1, Pallas kernels: 176 us -> 176 us  [gather_all(): pl.pallas_call(functools.partial(gather_kernel, shards), out_shape=jax.Sh...]
  transfers between devices with their start and end apart: 1 -> 0, of which waited for: 0 -> 0; matrix products, arithmetic and copies ran while one was open for 2% -> 0% of each run, Pallas kernels for 0% -> 0%
where the time goes in v2:
time: 236 us; the launch traced here: 232 us
  Pallas kernels  221 us (94%)
  local copies, waits for them, and re-layouts  7.56 us (3%)
  other arithmetic  3.29 us (1%)
    pallas_call x1, Pallas kernels, gather_all(): pl.pallas_call(functools.partial(gather_kernel, shards), out_shape=jax.Sh...  176 us
    pallas_call x1, Pallas kernels, scatter_all(): pl.pallas_call(functools.partial(scatter_kernel, shards), out_shape=jax.S...  30.9 us
    pallas_call x1, Pallas kernels, attend_all(): pl.pallas_call(attend_kernel, grid_spec=pltpu.PrefetchScalarGridSpec(num_...  14.9 us
    unnamed x11, local copies, waits for them, and re-layouts  6.81 us

profile of v2, /device:TPU:8, one launch (start us, length us, event | category | flops | bytes accessed | tf_op | source)
XLA Modules:
  0.0 232.4 jit_solution(11376333290343621399)
XLA Ops:
  0.0 0.9 convert_reduce_fusion.first
  0.9 0.8 select_reduce_fusion.1
  1.7 0.7 pad_maximum_fusion.gains
  2.4 0.1 iota_compare_fusion
  2.4 0.8 select_reduce_fusion.block_turn
  3.3 0.8 reshape.47.norm_gain
  4.1 0.0 copy-start.1
  4.1 1.3 copy-done.1
  5.4 0.0 copy-start.2
  5.4 1.3 copy-done.2
  6.7 0.0 copy-start.3
  6.7 0.9 copy-done.3
  7.6 0.0 copy-start.4
  7.6 175.7 %gather_all.1.q_ref.all_ref = bf16[2048,512]{1,0:T(8,128)(2,1)S(1)} custom-call(bf16[2,4,64,2688]{3,2,1,0:T(8,128)(2,1)} %bitcast.8, f32[2,2688]{1,0:T(2,128)S(1)} %reshape.47.norm_gain, f32[2,128]{1,0:T(2,128)S(1)} %pad_maximum_fusion.gains, f32[2,16,128]{2,1,0:T(8,128)S(1)} %select_reduce_fusion.block_turn, f32[2,128,128]{2,1,0:T(8,128)S(1)} %copy-done.3, ...), custom_call_target="tpu_custom_call" | custom-call | tf_op jit(solution)/shard_map/gather_all/pallas_call | solution.py:483
  183.3 0.0 copy-done.4
  183.4 14.9 %attend_all.1.result = bf16[2048,256]{1,0:T(8,128)(2,1)S(1)} custom-call(s32[16]{0:T(128)S(1)} %convert_reduce_fusion.first, s32[16]{0:T(128)S(1)} %copy-done.4, bf16[2048,512]{1,0:T(8,128)(2,1)S(1)} %gather_all.1.q_ref.all_ref, bf16[2048,512]{1,0:T(8,128)(2,1)S(1)} %gather_all.1.q_ref.all_ref), custom_call_target="tpu_custom_call" | custom-call | tf_op jit(solution)/shard_map/attend_all/pallas_call | solution.py:553
  198.3 0.0 copy-start
  198.3 1.0 copy-done
  199.3 30.9 %scatter_all.1 = bf16[512,1024]{1,0:T(8,128)(2,1)} custom-call(bf16[2048,256]{1,0:T(8,128)(2,1)} %copy-done), custom_call_target="tpu_custom_call" | custom-call | tf_op jit(solution)/shard_map/scatter_all/pallas_call | solution.py:613
  230.1 2.3 copy.13
  (1 shorter events, 0.0 us)
Async XLA Ops:
  4.1 1.3 copy-start.1
  5.4 1.3 copy-start.2
  6.7 0.9 copy-start.3
  7.6 175.7 %copy-start.4 = (s32[16]{0:T(128)S(1)}, s32[16]{0:T(128)}, u32[]{:S(2)}) copy-start(s32[16]{0:T(128)} %source.1) | copy-start | bytes 196
  198.3 1.0 copy-start

commit v3 on v2

--- a/solution.py
+++ b/solution.py
@@ -324,12 +324,6 @@
     def sums():
         return remote(mine, theirs, s_send, s_recv, sub=1 - c)
 
-    for d in range(1, shards):
-        for n in range(3):
-            weight_piece(d, n).start()
-    for n in range(3):
-        own_weight(n).start()
-
     def add_up(i, _):
         half, j = i // chunks, i % chunks
         values = hidden[half, j].astype(jnp.float32)
@@ -356,6 +350,11 @@
         return 0
 
     lax.fori_loop(0, 2 * chunks, normalise, 0)
+    for d in range(1, shards):
+        for n in range(3):
+            weight_piece(d, n).start()
+    for n in range(3):
+        own_weight(n).start()
 
     def has(step, right):
         return z - step >= 0 if right else z + step < shards

time: 236 us -> 229 us (0.970)
  Pallas kernels: 221 us -> 217 us
    pallas_call x1, Pallas kernels: 176 us -> 162 us  [gather_all(): pl.pallas_call(functools.partial(gather_kernel, shards), out_shape=jax.Sh...]
    pallas_call x1, Pallas kernels: 30.9 us -> 39.6 us  [scatter_all(): pl.pallas_call(functools.partial(scatter_kernel, shards), out_shape=jax.S...]
where the time goes in v3:
time: 229 us; the launch traced here: 227 us
  Pallas kernels  217 us (95%)
  local copies, waits for them, and re-layouts  7.56 us (3%)
  other arithmetic  3.29 us (1%)
    pallas_call x1, Pallas kernels, gather_all(): pl.pallas_call(functools.partial(gather_kernel, shards), out_shape=jax.Sh...  162 us
    pallas_call x1, Pallas kernels, scatter_all(): pl.pallas_call(functools.partial(scatter_kernel, shards), out_shape=jax.S...  39.6 us
    pallas_call x1, Pallas kernels, attend_all(): pl.pallas_call(attend_kernel, grid_spec=pltpu.PrefetchScalarGridSpec(num_...  14.9 us
    unnamed x11, local copies, waits for them, and re-layouts  6.81 us

profile of v3, /device:TPU:8, one launch (start us, length us, event | category | flops | bytes accessed | tf_op | source)
XLA Modules:
  0.0 227.4 jit_solution(18237667453927891295)
XLA Ops:
  0.0 0.9 convert_reduce_fusion.first
  0.9 0.8 select_reduce_fusion.1
  1.7 0.7 pad_maximum_fusion.gains
  2.4 0.1 iota_compare_fusion
  2.4 0.8 select_reduce_fusion.block_turn
  3.3 0.8 reshape.47.norm_gain
  4.1 0.0 copy-start.1
  4.1 1.3 copy-done.1
  5.4 0.0 copy-start.2
  5.4 1.3 copy-done.2
  6.7 0.0 copy-start.3
  6.7 0.9 copy-done.3
  7.6 0.0 copy-start.4
  7.6 162.0 %gather_all.1.q_ref.all_ref = bf16[2048,512]{1,0:T(8,128)(2,1)S(1)} custom-call(bf16[2,4,64,2688]{3,2,1,0:T(8,128)(2,1)} %bitcast.8, f32[2,2688]{1,0:T(2,128)S(1)} %reshape.47.norm_gain, f32[2,128]{1,0:T(2,128)S(1)} %pad_maximum_fusion.gains, f32[2,16,128]{2,1,0:T(8,128)S(1)} %select_reduce_fusion.block_turn, f32[2,128,128]{2,1,0:T(8,128)S(1)} %copy-done.3, ...), custom_call_target="tpu_custom_call" | custom-call | tf_op jit(solution)/shard_map/gather_all/pallas_call | solution.py:482
  169.6 0.0 copy-done.4
  169.7 14.9 %attend_all.1.result = bf16[2048,256]{1,0:T(8,128)(2,1)S(1)} custom-call(s32[16]{0:T(128)S(1)} %convert_reduce_fusion.first, s32[16]{0:T(128)S(1)} %copy-done.4, bf16[2048,512]{1,0:T(8,128)(2,1)S(1)} %gather_all.1.q_ref.all_ref, bf16[2048,512]{1,0:T(8,128)(2,1)S(1)} %gather_all.1.q_ref.all_ref), custom_call_target="tpu_custom_call" | custom-call | tf_op jit(solution)/shard_map/attend_all/pallas_call | solution.py:552
  184.6 0.0 copy-start
  184.6 1.0 copy-done
  185.6 39.6 %scatter_all.1 = bf16[512,1024]{1,0:T(8,128)(2,1)} custom-call(bf16[2048,256]{1,0:T(8,128)(2,1)} %copy-done), custom_call_target="tpu_custom_call" | custom-call | tf_op jit(solution)/shard_map/scatter_all/pallas_call | solution.py:612
  225.2 2.3 copy.13
  (1 shorter events, 0.0 us)
Async XLA Ops:
  4.1 1.3 copy-start.1
  5.4 1.3 copy-start.2
  6.7 0.9 copy-start.3
  7.6 162.0 %copy-start.4 = (s32[16]{0:T(128)S(1)}, s32[16]{0:T(128)}, u32[]{:S(2)}) copy-start(s32[16]{0:T(128)} %source.1) | copy-start | bytes 196
  184.6 1.0 copy-start
